TPU v7x, 256 devices: a whole 4x4x8 slice. The times are simulated.
256 devices in a mesh: row: 8 (over z), col: 16 (over x, y_lo, core), rep: 2 (over y_hi).
Axes of the slice: x: 4, y: 4 (y_hi: 2, y_lo: 2; y = y_hi * 2 + y_lo), z: 8, core: 2. Of those that a mesh axis runs over, the one named last changes fastest.
Arguments:
- a_blocks: bfloat16 [16384, 4096], P('row', 'col'), may hold values from -6 to 6
- a_mask: int32 [64, 16], P('row', 'col'), may hold values from 0 to 1, as said below
- b_blocks: bfloat16 [4096, 8192], P('row', 'col'), may hold values from -0.09375 to 0.09375
- b_mask: int32 [16, 32], P('row', 'col'), may hold values from 0 to 1
Outputs:
- c_product: bfloat16 [16384, 8192], P('row', ('col', 'rep'))
Inputs may be any that keep to these rules, and one draw needn't show every extreme that they name: a_mask holds 0 or 1; within each aligned tile of 8 block rows by 1 inner blocks (one device's tile) at most 2 entries are 1, and some tile holds exactly 2.
All inputs are finite; a program needn't handle non-finite values.
Results may differ from a plain program's by a relative error of at most 0.007.
Values may be sent and summed in bfloat16 or wider, within the bound.
A program may use at most 64 MiB of HBM per device.

v0:
```python
import jax
import jax.numpy as jnp
from jax import lax
from jax.sharding import PartitionSpec as P

BS = 256


def from_everyone(shard, axis):
    length = lax.axis_size(axis)
    return lax.all_to_all(
        jnp.broadcast_to(shard[None], (length, *shard.shape)), axis, 0, 0, tiled=True
    )


def in_order(pieces, dim):
    pieces = jnp.moveaxis(pieces, 0, dim)
    shape = pieces.shape
    return pieces.reshape(*shape[:dim], shape[dim] * shape[dim + 1], *shape[dim + 2 :])


def gather_directly(shard, axis, dim):
    pieces = from_everyone(shard, axis)
    return in_order(pieces, dim)


def expand(values, pattern):
    block_rows = pattern.shape[0]
    block_cols = pattern.shape[1]
    shaped = values.reshape(block_rows, BS, block_cols, BS) * pattern[:, None, :, None].astype(
        jnp.bfloat16
    )
    return shaped.reshape(block_rows * BS, block_cols * BS)


def pack_blocks(a_blocks, a_mask):
    block_rows = a_mask.shape[0]
    block_cols = a_mask.shape[1]
    slot_count = max(block_rows // 4, 1)
    flat_mask = a_mask.reshape(-1)
    slot_of = jnp.cumsum(flat_mask) - 1
    slot_ids = jnp.arange(slot_count, dtype=jnp.int32)[:, None]
    chosen = (flat_mask[None, :] == 1) & (slot_of[None, :] == slot_ids)
    flat_blocks = (
        a_blocks.reshape(block_rows, BS, block_cols, BS)
        .transpose(0, 2, 1, 3)
        .reshape(block_rows * block_cols, BS * BS)
    )
    packed = jnp.dot(
        chosen.astype(jnp.bfloat16), flat_blocks, preferred_element_type=jnp.float32
    ).astype(jnp.bfloat16)
    positions = jnp.arange(block_rows * block_cols, dtype=jnp.int32)
    chosen_int = chosen.astype(jnp.int32)
    used = jnp.sum(chosen_int, axis=1) > 0
    block_row = jnp.where(
        used, jnp.sum(chosen_int * (positions // block_cols)[None, :], axis=1), block_rows
    )
    block_inner = jnp.where(
        used, jnp.sum(chosen_int * (positions % block_cols)[None, :], axis=1), 0
    )
    codes = jnp.stack([block_row, block_inner], axis=1)
    return (packed.reshape(slot_count, BS, BS), codes)


def per_device(a_blocks, a_mask, b_blocks, b_mask):
    masked_b = expand(b_blocks, b_mask)
    layer_index = lax.axis_index("rep")
    c_width = masked_b.shape[1]
    own_width = c_width // 2
    own_b = lax.dynamic_slice_in_dim(masked_b, layer_index * own_width, own_width, 1)
    column_b = gather_directly(own_b, "row", 0)
    row_count = a_blocks.shape[0]
    block_rows = a_mask.shape[0]
    inner_local = a_mask.shape[1]
    inner_total = column_b.shape[0] // BS
    stacked_b = column_b.reshape(inner_total, BS, own_width)
    packed, codes = pack_blocks(a_blocks, a_mask)
    slot_count = packed.shape[0]
    row_ids = jnp.arange(block_rows, dtype=jnp.int32)
    blocks = lax.all_gather(packed, "col", axis=0, tiled=True)
    block_codes = lax.all_gather(codes, "col", axis=0, tiled=True)
    item_count = blocks.shape[0]
    owner = jnp.arange(item_count, dtype=jnp.int32) // slot_count
    inner = (owner * inner_local + block_codes[:, 1]).astype(jnp.int32)
    picked = jnp.take(stacked_b, inner, axis=0)
    partial_blocks = jnp.einsum("sij,sjn->sin", blocks, picked, preferred_element_type=jnp.float32)
    selector = (block_codes[:, 0][:, None] == row_ids[None, :]).astype(jnp.float32)
    summed = jnp.einsum("sr,sin->rin", selector, partial_blocks)
    product = summed.reshape(row_count, own_width)
    return product.astype(jnp.bfloat16)


def solution(mesh):
    in_specs = (P("row", "col"), P("row", "col"), P("row", "col"), P("row", "col"))
    out_specs = P("row", ("col", "rep"))
    return jax.shard_map(
        per_device, mesh=mesh, in_specs=in_specs, out_specs=out_specs, check_vma=False
    )
```

profile of v0, /device:TPU:4, one launch (start us, length us, event | category | flops | bytes accessed | tf_op | source)
XLA Modules:
  0.0 90.8 jit_solution(8333974112397646809)
XLA Ops:
  6.5 0.0 copy-start.1
  6.5 0.0 copy-start
  6.5 0.0 all-gather.3.cloned.1.call-start
  6.5 0.7 compare_bitcast_fusion
  7.3 0.8 reduce-window.8
  8.1 1.7 %reshape_transpose_reshape.3 = bf16[8,65536]{1,0:T(8,128)(2,1)S(1)} reshape(bf16[2048,256]{1,0:T(8,128)(2,1)} %param.4) | data formatting | bytes 2097152 | tf_op jit(solution)/shard_map/reshape;transpose;reshape | solution.py:47
  9.8 0.1 convert_reduce_fusion
  9.9 0.4 convolution_convert_fusion
  10.4 0.7 copy.29
  11.1 0.0 all-gather.3.cloned.1.call-update
  11.1 0.0 copy-done.1
  11.2 0.3 mul.31
  11.5 0.1 copy.23
  11.6 0.0 copy-done
  11.6 0.1 dynamic-slice_multiply_fusion
  11.7 1.5 %broadcast_in_dim.29 = bf16[8,512,256]{2,1,0:T(8,128)(2,1)} broadcast(bf16[512,256]{1,0:T(8,128)(2,1)S(1)} %dynamic-slice_multiply_fusion), dimensions={1,2} | broadcast | bytes 2359296 | tf_op jit(solution)/shard_map/broadcast_in_dim | solution.py:12
  13.2 8.5 %all-to-all-start = ((bf16[8,512,256]{2,1,0:T(8,128)(2,1)}), bf16[8,512,256]{2,1,0:T(8,128)(2,1)S(1)}, u32[]{:S(2)}, u32[]{:S(2)}) async-start(bf16[8,512,256]{2,1,0:T(8,128)(2,1)} %broadcast_in_dim.29), calls=%async_computation | async-start | bytes 4194304 | tf_op jit(solution)/shard_map/all_to_all | solution.py:11
  21.6 0.1 copy.21
  21.7 15.4 %all-gather = s32[16,2,2]{2,1,0:T(2,128)S(1)} all-gather(s32[1,2,2]{2,1,0:T(2,128)S(1)} %pad_bitcast_fusion), channel_id=1, replica_groups=mesh['row'=8,'col'=16,'rep'=2] {'col'}, dimensions={0}, use_global_device_ids=true | all-gather | bytes 272 | tf_op jit(solution)/shard_map/all_gather | solution.py:81
  37.1 0.1 fusion.15
  37.2 0.1 copy.19
  37.3 0.1 copy.20
  37.4 35.4 %all-to-all-done = bf16[8,512,256]{2,1,0:T(8,128)(2,1)S(1)} async-done(((bf16[8,512,256]{2,1,0:T(8,128)(2,1)}), bf16[8,512,256]{2,1,0:T(8,128)(2,1)S(1)}, u32[]{:S(2)}, u32[]{:S(2)}) %all-to-all-start) | async-done | bytes 2097184 | tf_op jit(solution)/shard_map/all_to_all | solution.py:11
  72.8 2.8 %gather_fusion = bf16[32,256,256]{2,1,0:T(8,128)(2,1)} fusion(bf16[16,256,256]{2,1,0:T(8,128)(2,1)S(1)} %bitcast.28, s32[1024]{0:T(1024)S(1)} %pad_clamp_fusion), kind=kCustom, calls=%fused_computation | custom fusion | bytes 8388736 | tf_op jit(solution)/shard_map/jit(_take)/gather | solution.py:85
  75.6 0.0 all-gather.3.cloned.1.call-done
  75.6 4.8 %fusion.2 = bf16[32,256,256]{2,1,0:T(8,128)(2,1)S(1)} fusion(bf16[32,256,256]{2,1,0:T(8,128)(2,1)} %all-gather.3.cloned.1.call-done, bf16[32,256,256]{2,1,0:T(8,128)(2,1)} %gather_fusion, pred[32]{0:T(512)(128)(4,1)S(1)} %get-tuple-element.7), kind=kOutput, calls=%fused_computation.4 | convolution fusion | flops 1075838976 | bytes 12582944 | tf_op jit(solution)/shard_map/sij,sjn->sin/dot_general | solution.py:86
  80.4 2.4 %fusion.6 = bf16[8,256,256]{2,0,1:T(8,128)(2,1)S(1)} fusion(bf16[32,256,256]{2,1,0:T(8,128)(2,1)S(1)} %fusion.2, s32[32]{0:T(128)S(1)} %bitcast.34), kind=kOutput, calls=%fused_computation.8 | convolution fusion | flops 33554688 | bytes 5243008 | tf_op jit(solution)/shard_map/sr,sin->rin/dot_general | solution.py:88
  82.8 1.2 %copy.17 = bf16[8,256,256]{2,1,0:T(8,128)(2,1)} copy(bf16[8,256,256]{2,0,1:T(8,128)(2,1)S(1)} %fusion.6) | data formatting | bytes 2097152 | tf_op jit(solution)/shard_map/convert_element_type | solution.py:90
  (6 shorter events, 0.0 us)
Async XLA Ops:
  6.5 4.6 %copy-start.1 = (s32[2,2]{1,0:T(2,128)S(1)}, s32[2,2]{1,0:T(2,128)}, u32[]{:S(2)}) copy-start(s32[2,2]{1,0:T(2,128)} %param.7) | copy-start | bytes 52
  6.5 5.1 %copy-start = (bf16[512,512]{1,0:T(8,128)(2,1)S(1)}, bf16[512,512]{1,0:T(8,128)(2,1)}, u32[]{:S(2)}) copy-start(bf16[512,512]{1,0:T(8,128)(2,1)} %param.6) | copy-start | bytes 1572868
  6.5 69.1 %all-gather.3.cloned.1.call-start = ((), (), s32[]{:S(2)}) async-start(), calls=%async_computation.1 | async-start | bytes 4456448 | tf_op jit(solution)/shard_map/all_gather | solution.py:80
  13.2 59.7 %all-to-all-start = ((bf16[8,512,256]{2,1,0:T(8,128)(2,1)}), bf16[8,512,256]{2,1,0:T(8,128)(2,1)S(1)}, u32[]{:S(2)}, u32[]{:S(2)}) async-start(bf16[8,512,256]{2,1,0:T(8,128)(2,1)} %broadcast_in_dim.29), calls=%async_computation | async-start | bytes 4194304 | tf_op jit(solution)/shard_map/all_to_all | solution.py:11
Sparse Core Ops, SparseCore 0:
  11.3 41.8 all-gather.2
where the time goes:
time: 91 us; the launch traced here: 90.8 us
  waiting for transfers between devices  35.4 us (39%)
  blocking collectives  15.4 us (17%)
  between operations  13.5 us (15%)
  local copies, waits for them, and re-layouts  8.6 us (9%)
  starting transfers between devices  8.47 us (9%)
  matrix products  7.58 us (8%)
  other arithmetic  1.81 us (2%)
    all_to_all x1, waiting for transfers between devices, from_everyone(): lax.all_to_all(jnp.broadcast_to(shard[None], (length, *shard.shape)), axi...  35.4 us
    all_gather x1, blocking collectives, per_device(): block_codes = lax.all_gather(codes, 'col', axis=0, tiled=True)  15.4 us
    all_to_all x1, starting transfers between devices, from_everyone(): lax.all_to_all(jnp.broadcast_to(shard[None], (length, *shard.shape)), axi...  8.47 us
    dot_general x1, matrix products, per_device(): jnp.einsum('sij,sjn->sin', blocks, picked, preferred_element_type=jnp.flo...  4.8 us
    gather x1, local copies, waits for them, and re-layouts, per_device(): picked = jnp.take(stacked_b, inner, axis=0)  2.77 us
    dot_general x1, matrix products, per_device(): summed = jnp.einsum('sr,sin->rin', selector, partial_blocks)  2.35 us
  transfers between devices with their start and end apart: 2, of which 1 were waited for; matrix products, arithmetic and copies ran while one was open for 6% of the time, Pallas kernels for 0%

commit v1 on v0

--- a/solution.py
+++ b/solution.py
@@ -4,6 +4,13 @@
 from jax.sharding import PartitionSpec as P
 
 BS = 256
+
+
+def clusters_handle(patch):
+    m_next = jnp.concatenate(
+        jax.lax.all_to_all(jnp.stack([patch] * jax.lax.axis_size("col")), "col", 0, 0), axis=0
+    )
+    return m_next
 
 
 def from_everyone(shard, axis):
@@ -78,7 +85,7 @@
     slot_count = packed.shape[0]
     row_ids = jnp.arange(block_rows, dtype=jnp.int32)
     blocks = lax.all_gather(packed, "col", axis=0, tiled=True)
-    block_codes = lax.all_gather(codes, "col", axis=0, tiled=True)
+    block_codes = clusters_handle(codes)
     item_count = blocks.shape[0]
     owner = jnp.arange(item_count, dtype=jnp.int32) // slot_count
     inner = (owner * inner_local + block_codes[:, 1]).astype(jnp.int32)

time: 91 us -> 103 us (1.13); the launches traced: 90.8 us -> 101 us
  waiting for transfers between devices: 35.4 us -> 54.6 us
  blocking collectives: 15.4 us -> 0 us
  starting transfers between devices: 8.47 us -> 14.3 us
    all_to_all x1, waiting for transfers between devices: 35.4 us -> 51.3 us  [from_everyone(): lax.all_to_all(jnp.broadcast_to(shard[None], (length, *shard.shape)), axi...]
    all_gather x1 -> x0, blocking collectives: 15.4 us -> none  [per_device(): block_codes = lax.all_gather(codes, 'col', axis=0, tiled=True)]
    all_to_all x0 -> x1, starting transfers between devices: none -> 5.84 us  [clusters_handle(): jax.lax.all_to_all(jnp.stack([patch] * jax.lax.axis_size('col')), 'col',...]
    all_to_all x0 -> x1, waiting for transfers between devices: none -> 3.29 us  [clusters_handle(): jax.lax.all_to_all(jnp.stack([patch] * jax.lax.axis_size('col')), 'col',...]
  transfers between devices with their start and end apart: 2 -> 3, of which waited for: 1 -> 2; matrix products, arithmetic and copies ran while one was open for 6% -> 5% of each run, Pallas kernels for 0% -> 0%
where the time goes in v1:
time: 103 us; the launch traced here: 101 us
  waiting for transfers between devices  54.6 us (53%)
  starting transfers between devices  14.3 us (14%)
  between operations  13.5 us (13%)
  local copies, waits for them, and re-layouts  8.98 us (9%)
  matrix products  7.58 us (7%)
  other arithmetic  1.81 us (2%)
    all_to_all x1, waiting for transfers between devices, from_everyone(): lax.all_to_all(jnp.broadcast_to(shard[None], (length, *shard.shape)), axi...  51.3 us
    all_to_all x1, starting transfers between devices, from_everyone(): lax.all_to_all(jnp.broadcast_to(shard[None], (length, *shard.shape)), axi...  8.47 us
    all_to_all x1, starting transfers between devices, clusters_handle(): jax.lax.all_to_all(jnp.stack([patch] * jax.lax.axis_size('col')), 'col',...  5.84 us
    dot_general x1, matrix products, per_device(): jnp.einsum('sij,sjn->sin', blocks, picked, preferred_element_type=jnp.flo...  4.8 us
    all_to_all x1, waiting for transfers between devices, clusters_handle(): jax.lax.all_to_all(jnp.stack([patch] * jax.lax.axis_size('col')), 'col',...  3.29 us
    gather x1, local copies, waits for them, and re-layouts, per_device(): picked = jnp.take(stacked_b, inner, axis=0)  2.79 us
    dot_general x1, matrix products, per_device(): summed = jnp.einsum('sr,sin->rin', selector, partial_blocks)  2.35 us
  transfers between devices with their start and end apart: 3, of which 2 were waited for; matrix products, arithmetic and copies ran while one was open for 5% of the time, Pallas kernels for 0%

profile of v1, /device:TPU:4, one launch (start us, length us, event | category | flops | bytes accessed | tf_op | source)
XLA Modules:
  0.0 100.8 jit_solution(3396335847836139862)
XLA Ops:
  6.5 0.0 copy-start.1
  6.5 0.0 copy-start
  6.5 0.0 all-gather.2.cloned.1.call-start
  6.5 0.7 compare_bitcast_fusion
  7.3 0.8 reduce-window.8
  8.1 1.7 %reshape_transpose_reshape.3 = bf16[8,65536]{1,0:T(8,128)(2,1)S(1)} reshape(bf16[2048,256]{1,0:T(8,128)(2,1)} %param.4) | data formatting | bytes 2097152 | tf_op jit(solution)/shard_map/reshape;transpose;reshape | solution.py:54
  9.8 0.1 convert_reduce_fusion
  9.9 0.4 convolution_convert_fusion
  10.4 0.7 copy.19
  11.1 0.0 all-gather.2.cloned.1.call-update
  11.2 0.6 stack.5
  11.8 5.8 %all-to-all-start = ((s32[16,2,2]{1,2,0:T(2,128)}), s32[16,2,2]{1,2,0:T(2,128)S(1)}, u32[]{:S(2)}, u32[]{:S(2)}) async-start(s32[16,2,2]{1,2,0:T(2,128)} %stack.5), calls=%async_computation | async-start | bytes 32768 | tf_op jit(solution)/shard_map/all_to_all | solution.py:11
  17.6 0.0 copy-done.1
  17.6 0.3 mul.31
  18.0 0.1 copy.13
  18.1 0.0 copy-done
  18.1 0.1 dynamic-slice_multiply_fusion
  18.2 3.3 %all-to-all-done = s32[16,2,2]{1,2,0:T(2,128)S(1)} async-done(((s32[16,2,2]{1,2,0:T(2,128)}), s32[16,2,2]{1,2,0:T(2,128)S(1)}, u32[]{:S(2)}, u32[]{:S(2)}) %all-to-all-start) | async-done | bytes 288 | tf_op jit(solution)/shard_map/all_to_all | solution.py:11
  21.4 1.5 %broadcast_in_dim.29 = bf16[8,512,256]{2,1,0:T(8,128)(2,1)} broadcast(bf16[512,256]{1,0:T(8,128)(2,1)S(1)} %dynamic-slice_multiply_fusion), dimensions={1,2} | broadcast | bytes 2359296 | tf_op jit(solution)/shard_map/broadcast_in_dim | solution.py:19
  22.9 8.5 %all-to-all-start.1 = ((bf16[8,512,256]{2,1,0:T(8,128)(2,1)}), bf16[8,512,256]{2,1,0:T(8,128)(2,1)S(1)}, u32[]{:S(2)}, u32[]{:S(2)}) async-start(bf16[8,512,256]{2,1,0:T(8,128)(2,1)} %broadcast_in_dim.29), calls=%async_computation.1 | async-start | bytes 4194304 | tf_op jit(solution)/shard_map/all_to_all | solution.py:18
  31.4 0.1 reshape.111
  31.5 51.3 %all-to-all-done.1 = bf16[8,512,256]{2,1,0:T(8,128)(2,1)S(1)} async-done(((bf16[8,512,256]{2,1,0:T(8,128)(2,1)}), bf16[8,512,256]{2,1,0:T(8,128)(2,1)S(1)}, u32[]{:S(2)}, u32[]{:S(2)}) %all-to-all-start.1) | async-done | bytes 2097184 | tf_op jit(solution)/shard_map/all_to_all | solution.py:18
  82.8 2.8 %gather_fusion = bf16[32,256,256]{2,1,0:T(8,128)(2,1)} fusion(bf16[16,256,256]{2,1,0:T(8,128)(2,1)S(1)} %bitcast.28, s32[1024]{0:T(1024)S(1)} %pad_clamp_fusion), kind=kCustom, calls=%fused_computation | custom fusion | bytes 8388736 | tf_op jit(solution)/shard_map/jit(_take)/gather | solution.py:92
  85.6 0.0 all-gather.2.cloned.1.call-done
  85.6 4.8 %fusion.2 = bf16[32,256,256]{2,1,0:T(8,128)(2,1)S(1)} fusion(bf16[32,256,256]{2,1,0:T(8,128)(2,1)} %all-gather.2.cloned.1.call-done, bf16[32,256,256]{2,1,0:T(8,128)(2,1)} %gather_fusion, pred[32]{0:T(512)(128)(4,1)S(1)} %get-tuple-element.7), kind=kOutput, calls=%fused_computation.4 | convolution fusion | flops 1075838976 | bytes 12582944 | tf_op jit(solution)/shard_map/sij,sjn->sin/dot_general | solution.py:93
  90.4 2.4 %fusion.6 = bf16[8,256,256]{2,0,1:T(8,128)(2,1)S(1)} fusion(bf16[32,256,256]{2,1,0:T(8,128)(2,1)S(1)} %fusion.2, s32[32]{0:T(128)S(1)} %slice_bitcast_fusion), kind=kOutput, calls=%fused_computation.8 | convolution fusion | flops 33554688 | bytes 5243008 | tf_op jit(solution)/shard_map/sr,sin->rin/dot_general | solution.py:95
  92.8 1.2 %copy.11 = bf16[8,256,256]{2,1,0:T(8,128)(2,1)} copy(bf16[8,256,256]{2,0,1:T(8,128)(2,1)S(1)} %fusion.6) | data formatting | bytes 2097152 | tf_op jit(solution)/shard_map/convert_element_type | solution.py:97
  (8 shorter events, 0.0 us)
Async XLA Ops:
  6.5 11.1 %copy-start.1 = (s32[2,2]{1,0:T(2,128)S(1)}, s32[2,2]{1,0:T(2,128)}, u32[]{:S(2)}) copy-start(s32[2,2]{1,0:T(2,128)} %param.7) | copy-start | bytes 52
  6.5 11.5 %copy-start = (bf16[512,512]{1,0:T(8,128)(2,1)S(1)}, bf16[512,512]{1,0:T(8,128)(2,1)}, u32[]{:S(2)}) copy-start(bf16[512,512]{1,0:T(8,128)(2,1)} %param.6) | copy-start | bytes 1572868
  6.5 79.1 %all-gather.2.cloned.1.call-start = ((), (), s32[]{:S(2)}) async-start(), calls=%async_computation.2 | async-start | bytes 4456448 | tf_op jit(solution)/shard_map/all_gather | solution.py:87
  11.8 9.7 %all-to-all-start = ((s32[16,2,2]{1,2,0:T(2,128)}), s32[16,2,2]{1,2,0:T(2,128)S(1)}, u32[]{:S(2)}, u32[]{:S(2)}) async-start(s32[16,2,2]{1,2,0:T(2,128)} %stack.5), calls=%async_computation | async-start | bytes 32768 | tf_op jit(solution)/shard_map/all_to_all | solution.py:11
  22.9 59.9 %all-to-all-start.1 = ((bf16[8,512,256]{2,1,0:T(8,128)(2,1)}), bf16[8,512,256]{2,1,0:T(8,128)(2,1)S(1)}, u32[]{:S(2)}, u32[]{:S(2)}) async-start(bf16[8,512,256]{2,1,0:T(8,128)(2,1)} %broadcast_in_dim.29), calls=%async_computation.1 | async-start | bytes 4194304 | tf_op jit(solution)/shard_map/all_to_all | solution.py:18
Sparse Core Ops, SparseCore 0:
  11.3 41.8 all-gather.1
